TPU v7x, 512 devices: a whole 4x8x8 slice. The times are simulated.
512 devices in a mesh: phase: 8 (over z), ctx: 64 (over x, y, core).
Axes of the slice: x: 4, y: 8, z: 8, core: 2. Of those that a mesh axis runs over, the one named last changes fastest.
Arguments:
- activations: bfloat16 [8, 8192, 4096], P('phase', 'ctx'), may hold values from -6 to 6
- norm_gain: bfloat16 [8, 4096], P('phase'), may hold values from 0.25 to 1.75
- short_taps: bfloat16 [8, 3, 3, 4096], P('phase'), may hold values from -3 to 3
- skip_gain: bfloat16 [8, 4096], P('phase'), may hold values from 0.19921875 to 1.5
- time_const: float32 [8, 4096, 16], P('phase', 'ctx'), may hold values from 25 to 32768
- residues: float32 [8, 4096, 16], P('phase', 'ctx'), may hold values from -2 to 2
Outputs:
- handed: bfloat16 [8, 8192, 4096], P('phase', 'ctx')
All inputs are finite; a program needn't handle non-finite values.
Results may differ from a plain program's by a relative error of at most 0.0058.
Values may be sent and summed in bfloat16 or wider, within the bound.
A program may use at most 128 MiB of HBM per device.

v0:
```python
import math
import jax
import jax.numpy as jnp
from jax import lax
from jax.sharding import PartitionSpec as P

HIGHEST_PRECISION = lax.Precision.HIGHEST


def from_behind(shard, axis, by):
    count = lax.axis_size(axis)
    pairs = [(i, i + by) for i in range(count) if 0 <= i + by < count]
    return lax.ppermute(shard, axis, pairs)


def from_behind_2(block, axis, distance):
    devices = range(lax.axis_size(axis))
    route = [((i - distance) % len(devices), i) for i in devices]
    return lax.ppermute(block, axis, route)


def circle_angle(product, modulus):
    return 2.0 * math.pi / modulus * (product % modulus).astype(jnp.float32)


def filter_spectrum(decay_time, residue, frequency, padded_length, length):
    theta = circle_angle(frequency, padded_length)
    half_sine = jnp.sin(0.5 * theta)[None]
    full_sine = jnp.sin(theta)[None]
    parity = (1 - 2 * (frequency % 2)).astype(jnp.float32)[None]
    shape = (decay_time.shape[0],) + frequency.shape
    real_part = jnp.zeros(shape, jnp.float32)
    imag_part = jnp.zeros(shape, jnp.float32)
    for mode in range(decay_time.shape[1]):
        decay_rate = 1.0 / decay_time[:, mode][:, None, None]
        damping = jnp.exp(-decay_rate)
        leftover = -jnp.expm1(-decay_rate)
        weight = residue[:, mode][:, None, None] * jnp.sqrt(-jnp.expm1(-2.0 * decay_rate))
        numerator = weight * (1.0 - jnp.exp(-decay_rate * length) * parity)
        denom_real = leftover + 2.0 * damping * half_sine * half_sine
        denom_imag = damping * full_sine
        magnitude = denom_real * denom_real + denom_imag * denom_imag
        real_part = real_part + numerator * denom_real / magnitude
        imag_part = imag_part - numerator * denom_imag / magnitude
    return (real_part, imag_part)


def spectral_conv(mixed_in, decay_time, residue):
    devices = lax.axis_size("ctx")
    length, channels = mixed_in.shape
    local_channels = channels // devices
    sequence = length * devices
    pieces = jnp.transpose(mixed_in).reshape(devices, local_channels, length)
    lines = lax.all_to_all(pieces, "ctx", split_axis=0, concat_axis=2, tiled=True)[0]
    col_count = 128
    padded_length = 2 * sequence
    row_count = padded_length // col_count
    used_rows = row_count // 2
    row_index = jnp.arange(row_count, dtype=jnp.int32)
    used_index = jnp.arange(used_rows, dtype=jnp.int32)
    col_index = jnp.arange(col_count, dtype=jnp.int32)
    row_angle = circle_angle(row_index[:, None] * used_index[None, :], row_count)
    cos_rows = jnp.cos(row_angle)
    sin_rows = jnp.sin(row_angle)
    turn_angle = circle_angle(row_index[:, None] * col_index[None, :], padded_length)
    cos_turn = jnp.cos(turn_angle)
    sin_turn = jnp.sin(turn_angle)
    col_angle = circle_angle(col_index[:, None] * col_index[None, :], col_count)
    cos_cols = jnp.cos(col_angle)
    sin_cols = jnp.sin(col_angle)
    frequency = row_index[:, None] + row_count * col_index[None, :]
    group_size = math.gcd(local_channels, 16)
    group_count = local_channels // group_size
    mode_count = decay_time.shape[1]

    def one_group(parts):
        signal_part, time_part, residue_part = parts
        signal = signal_part.astype(jnp.float32)
        first_real = jnp.einsum("ka,cab->ckb", cos_rows, signal, precision=HIGHEST_PRECISION)
        first_imag = -jnp.einsum("ka,cab->ckb", sin_rows, signal, precision=HIGHEST_PRECISION)
        turned_real = first_real * cos_turn + first_imag * sin_turn
        turned_imag = first_imag * cos_turn - first_real * sin_turn
        freq_real = jnp.einsum(
            "ckb,bq->ckq", turned_real, cos_cols, precision=HIGHEST_PRECISION
        ) + jnp.einsum("ckb,bq->ckq", turned_imag, sin_cols, precision=HIGHEST_PRECISION)
        freq_imag = jnp.einsum(
            "ckb,bq->ckq", turned_imag, cos_cols, precision=HIGHEST_PRECISION
        ) - jnp.einsum("ckb,bq->ckq", turned_real, sin_cols, precision=HIGHEST_PRECISION)
        filt_real, filt_imag = filter_spectrum(
            time_part, residue_part, frequency, padded_length, sequence
        )
        prod_real = freq_real * filt_real - freq_imag * filt_imag
        prod_imag = freq_real * filt_imag + freq_imag * filt_real
        back_real = jnp.einsum(
            "ckq,bq->ckb", prod_real, cos_cols, precision=HIGHEST_PRECISION
        ) - jnp.einsum("ckq,bq->ckb", prod_imag, sin_cols, precision=HIGHEST_PRECISION)
        back_imag = jnp.einsum(
            "ckq,bq->ckb", prod_imag, cos_cols, precision=HIGHEST_PRECISION
        ) + jnp.einsum("ckq,bq->ckb", prod_real, sin_cols, precision=HIGHEST_PRECISION)
        spun_real = back_real * cos_turn - back_imag * sin_turn
        spun_imag = back_imag * cos_turn + back_real * sin_turn
        values = jnp.einsum(
            "ka,ckb->cab", cos_rows, spun_real, precision=HIGHEST_PRECISION
        ) - jnp.einsum("ka,ckb->cab", sin_rows, spun_imag, precision=HIGHEST_PRECISION)
        return (values / padded_length).astype(jnp.bfloat16)

    grouped_lines = lines.reshape(group_count, group_size, used_rows, col_count)
    time_groups = decay_time.reshape(group_count, group_size, mode_count)
    residue_groups = residue.reshape(group_count, group_size, mode_count)
    convolved = lax.map(one_group, (grouped_lines, time_groups, residue_groups))
    returned = lax.all_to_all(
        convolved.reshape(1, local_channels, sequence),
        "ctx",
        split_axis=2,
        concat_axis=0,
        tiled=True,
    )
    return jnp.transpose(returned.reshape(channels, length))


def local(activations, norm_gain, short_taps, skip_gain, time_const, residues):
    inputs = activations[0]
    length = inputs.shape[0]
    wide_in = inputs.astype(jnp.float32)
    square_mean = jnp.mean(wide_in * wide_in, axis=-1, keepdims=True)
    normed = (wide_in * lax.rsqrt(square_mean + 1e-06) * norm_gain[0].astype(jnp.float32)).astype(
        jnp.bfloat16
    )
    earlier_rows = from_behind(normed[length - 2 :], "ctx", 1)
    padded = jnp.concatenate([earlier_rows, normed], axis=0)
    wide_taps = short_taps[0].astype(jnp.float32)
    features = []
    for branch in range(3):
        total = jnp.zeros(inputs.shape, jnp.float32)
        for offset in range(3):
            total = total + wide_taps[branch, offset][None, :] * padded[
                2 - offset : 2 - offset + length
            ].astype(jnp.float32)
        features.append(total)
    query_feat, key_feat, value_feat = features
    mixed_in = (key_feat * value_feat).astype(jnp.bfloat16)
    conv_out = spectral_conv(mixed_in, time_const[0], residues[0])
    direct = skip_gain[0].astype(jnp.float32)[None, :] * mixed_in.astype(jnp.float32)
    block_out = (wide_in + query_feat * (conv_out.astype(jnp.float32) + direct)).astype(
        jnp.bfloat16
    )
    return from_behind_2(block_out[None], "phase", 1)


def solution(mesh):
    in_specs = (
        P("phase", "ctx", None),
        P("phase", None),
        P("phase", None, None, None),
        P("phase", None),
        P("phase", "ctx", None),
        P("phase", "ctx", None),
    )
    out_specs = P("phase", "ctx", None)
    return jax.shard_map(local, mesh=mesh, in_specs=in_specs, out_specs=out_specs, check_vma=False)
```

profile of v0, /device:TPU:1, one launch (start us, length us, event | category | flops | bytes accessed | tf_op | source)
XLA Modules:
  0.0 359.3 jit_solution(15073783701809906949)
XLA Ops:
  0.0 1.6 copy.105
  3.7 4.6 %collective-permute-start = (bf16[2,4096]{1,0:T(2,128)(2,1)S(1)}, bf16[2,4096]{1,0:T(2,128)(2,1)S(1)}, u32[]{:S(2)}, u32[]{:S(2)}) collective-permute-start(bf16[2,4096]{1,0:T(2,128)(2,1)S(1)} %copy.106), channel_id=1, source_target_pairs={{0,1},{1,2},{2,3},{3,4},{4,5},{5,6},{6,7},{7,8},{8,9},{9,10},{10,1... | collective-permute-start | bytes 49160 | tf_op jit(solution)/shard_map/ppermute | solution.py:13
  9.1 3.5 collective-permute-done
  13.1 5.6 %fusion.215 = bf16[128,4096]{0,1:T(8,128)(2,1)} fusion(bf16[128,4096]{0,1:T(8,128)(2,1)S(1)} %fusion.220, f32[4096]{0:T(1024)S(1)} %bitcast.389, f32[4096]{0:T(1024)S(1)} %bitcast.390, f32[4096]{0:T(1024)S(1)} %bitcast.391, f32[4096]{0:T(1024)S(1)} %bitcast.392, f32[4096]{0:T(1024)S(1)} %bitcast.393, f32[4096]{0:T(1024)S(1)} %bitcast.394, ...), kind=kLoop, calls=%fused_computation.400 | loop fusion | flops 11010048 | bytes 2211840 | tf_op jit(solution)/shard_map/convert_element_type | solution.py:141
  18.7 9.2 %all-to-all-start = ((bf16[64,64,128]{2,1,0:T(8,128)(2,1)}), bf16[64,64,128]{2,1,0:T(8,128)(2,1)}, u32[]{:S(2)}, u32[]{:S(2)}) async-start(bf16[64,64,128]{2,1,0:T(8,128)(2,1)} %bitcast.15), calls=%async_computation | async-start | bytes 2097152 | tf_op jit(solution)/shard_map/all_to_all | solution.py:54
  28.2 28.3 %all-to-all-done = bf16[64,64,128]{2,1,0:T(8,128)(2,1)} async-done(((bf16[64,64,128]{2,1,0:T(8,128)(2,1)}), bf16[64,64,128]{2,1,0:T(8,128)(2,1)}, u32[]{:S(2)}, u32[]{:S(2)}) %all-to-all-start) | async-done | bytes 1048608 | tf_op jit(solution)/shard_map/all_to_all | solution.py:54
  56.5 152.4 %while.18 = (s32[]{:T(128)}, bf16[4,16,64,128]{3,2,1,0:T(8,128)(2,1)}, bf16[4,16,64,128]{3,1,0,2:T(8,128)(2,1)}, f32[4,16,16]{1,0,2:T(4,128)S(1)}, f32[4,16,16]{1,0,2:T(4,128)S(1)}, /*index=5*/s32[128]{0:T(128)S(1)}, s32[]{:T(128)}) while((s32[]{:T(128)}, bf16[4,16,64,128]{3,2,1,0:T(8,128)(2,1)}, ...), condition=%wide.region_2.3_spmd.clone.clone.clone, body=%wide.region_1.2_spmd.clone.clone.clone.sunk | while | flops 4104389632 | bytes 44585556 | solution.py:110
  78.5 2.0 fusion.276
  80.5 2.0 convolution_add_fusion.4
  83.0 2.0 fusion.280
  85.6 12.2 %multiply_subtract_fusion.9 = (f32[16,128,128]{2,1,0:T(8,128)S(1)}, f32[16,128,128]{2,1,0:T(8,128)S(1)}, f32[16,128,128]{2,1,0:T(8,128)S(1)}, f32[16,128,128]{2,1,0:T(8,128)S(1)}) fusion(f32[16,128,128]{2,1,0:T(8,128)S(1)} %convolution_add_fusion.4, f32[16]{0:T(128)S(1)} %broadcast_multiply_fusion.32, f32[16]{0:T(128)S(1)} %get-tuple-element.1229, ...), kind=kOutput, calls=%fused_computation.108.clone.1 | convolution fusion | flops 471564288 | bytes 8721408 | tf_op jit(solution)/shard_map/while/body/eval_jaxpr/ckb,bq->ckq/dot_general | solution.py:88
  103.3 1.5 fusion.283
  104.8 2.2 fusion.284
  109.8 2.0 fusion.276
  111.8 2.0 convolution_add_fusion.4
  114.3 2.0 fusion.280
  116.9 12.2 %multiply_subtract_fusion.9 = (f32[16,128,128]{2,1,0:T(8,128)S(1)}, f32[16,128,128]{2,1,0:T(8,128)S(1)}, f32[16,128,128]{2,1,0:T(8,128)S(1)}, f32[16,128,128]{2,1,0:T(8,128)S(1)}) fusion(f32[16,128,128]{2,1,0:T(8,128)S(1)} %convolution_add_fusion.4, f32[16]{0:T(128)S(1)} %broadcast_multiply_fusion.32, f32[16]{0:T(128)S(1)} %get-tuple-element.1229, ...), kind=kOutput, calls=%fused_computation.108.clone.1 | convolution fusion | flops 471564288 | bytes 8721408 | tf_op jit(solution)/shard_map/while/body/eval_jaxpr/ckb,bq->ckq/dot_general | solution.py:88
  130.8 1.3 convolution_subtract_fusion.4
  133.4 1.3 convolution_add_fusion.5
  134.7 1.5 fusion.283
  136.1 2.2 fusion.284
  141.1 2.0 fusion.276
  143.1 2.0 convolution_add_fusion.4
  145.6 2.0 fusion.280
  148.3 12.2 %multiply_subtract_fusion.9 = (f32[16,128,128]{2,1,0:T(8,128)S(1)}, f32[16,128,128]{2,1,0:T(8,128)S(1)}, f32[16,128,128]{2,1,0:T(8,128)S(1)}, f32[16,128,128]{2,1,0:T(8,128)S(1)}) fusion(f32[16,128,128]{2,1,0:T(8,128)S(1)} %convolution_add_fusion.4, f32[16]{0:T(128)S(1)} %broadcast_multiply_fusion.32, f32[16]{0:T(128)S(1)} %get-tuple-element.1229, ...), kind=kOutput, calls=%fused_computation.108.clone.1 | convolution fusion | flops 471564288 | bytes 8721408 | tf_op jit(solution)/shard_map/while/body/eval_jaxpr/ckb,bq->ckq/dot_general | solution.py:88
  162.1 1.3 convolution_subtract_fusion.4
  164.7 1.3 convolution_add_fusion.5
  166.0 1.5 fusion.283
  167.5 2.2 fusion.284
  172.4 2.0 fusion.276
  174.4 2.0 convolution_add_fusion.4
  176.9 2.0 fusion.280
  179.6 12.2 %multiply_subtract_fusion.9 = (f32[16,128,128]{2,1,0:T(8,128)S(1)}, f32[16,128,128]{2,1,0:T(8,128)S(1)}, f32[16,128,128]{2,1,0:T(8,128)S(1)}, f32[16,128,128]{2,1,0:T(8,128)S(1)}) fusion(f32[16,128,128]{2,1,0:T(8,128)S(1)} %convolution_add_fusion.4, f32[16]{0:T(128)S(1)} %broadcast_multiply_fusion.32, f32[16]{0:T(128)S(1)} %get-tuple-element.1229, ...), kind=kOutput, calls=%fused_computation.108.clone.1 | convolution fusion | flops 471564288 | bytes 8721408 | tf_op jit(solution)/shard_map/while/body/eval_jaxpr/ckb,bq->ckq/dot_general | solution.py:88
  193.4 1.3 convolution_subtract_fusion.4
  197.3 1.5 fusion.283
  198.8 2.2 fusion.284
  208.9 1.5 reshape.1431
  210.4 6.8 %copy.111 = bf16[1,64,8192]{1,0,2:T(2,128)(2,1)} copy(bf16[1,64,8192]{2,1,0:T(8,128)(2,1)S(1)} %reshape.1431) | data formatting | bytes 2097152 | tf_op jit(solution)/shard_map/reshape | solution.py:112
  217.8 45.2 %reduce = bf16[8192,64]{1,0:T(8,128)(2,1)S(1)} reduce(bf16[8192,1,64]{2,1,0:T(2,128)(2,1)} %bitcast.378, bf16[]{:T(256)} %broadcast.1415), dimensions={1}, to_apply=%bitcast.256.reduce_sub_computation | reduce | bytes 2097154
  263.0 2.3 reshape.1506
  265.3 6.2 %all-to-all-start.1 = ((bf16[64,2,4096]{2,1,0:T(2,128)(2,1)}), bf16[64,2,4096]{2,1,0:T(2,128)(2,1)S(1)}, u32[]{:S(2)}, u32[]{:S(2)}) async-start(bf16[64,2,4096]{2,1,0:T(2,128)(2,1)} %reshape.1506), calls=%async_computation.1 | async-start | bytes 2097152 | tf_op jit(solution)/shard_map/all_to_all | solution.py:111
  271.5 28.5 %all-to-all-done.1 = bf16[64,2,4096]{2,1,0:T(2,128)(2,1)S(1)} async-done(((bf16[64,2,4096]{2,1,0:T(2,128)(2,1)}), bf16[64,2,4096]{2,1,0:T(2,128)(2,1)S(1)}, u32[]{:S(2)}, u32[]{:S(2)}) %all-to-all-start.1) | async-done | bytes 1048608 | tf_op jit(solution)/shard_map/all_to_all | solution.py:111
  300.1 7.0 %reshape.1507 = bf16[8192,1,64]{2,1,0:T(2,128)(2,1)} reshape(bf16[64,2,4096]{2,1,0:T(2,128)(2,1)S(1)} %all-to-all-done.1) | data formatting | bytes 2097152
  307.0 8.2 %copy.112 = bf16[1,64,8192]{2,1,0:T(8,128)(2,1)S(1)} copy(bf16[1,64,8192]{1,0,2:T(2,128)(2,1)} %bitcast.379) | data formatting | bytes 2097152 | tf_op jit(solution)/shard_map/all_to_all | solution.py:111
  317.6 6.1 %fusion.221 = bf16[128,4096]{0,1:T(8,128)(2,1)S(1)} fusion(bf16[128,4096]{0,1:T(8,128)(2,1)S(1)} %copy-done.3, f32[64,1,64,128]{3,2,0,1:T(8,128)S(1)} %copy.113, bf16[128,4096]{0,1:T(8,128)(2,1)} %fusion.215, bf16[1,128,4096]{1,2,0:T(8,128)(2,1)S(1)} %copy-done.1, f32[4096]{0:T(1024)S(1)} %bitcast.395, f32[4096]{0:T(1024)S(1)} %bitcast.387, ...), kind=kLoop, calls=%fused_computation.406 | loop fusion | flops 11010048 | bytes 6373376 | tf_op jit(solution)/shard_map/convert_element_type | solution.py:144
  323.7 4.0 %collective-permute-start.1 = (bf16[1,128,4096]{1,2,0:T(8,128)(2,1)S(1)}, bf16[1,128,4096]{1,2,0:T(8,128)(2,1)S(1)}, u32[]{:S(2)}, u32[]{:S(2)}) collective-permute-start(bf16[1,128,4096]{1,2,0:T(8,128)(2,1)S(1)} %bitcast.381), channel_id=1, source_target_pairs={{448,0},{0,64},{64,128},{128,192},{192,256},{256,320},{320,384},{3... | collective-permute-start | bytes 3145736 | tf_op jit(solution)/shard_map/ppermute | solution.py:19
  327.7 30.1 %collective-permute-done.1 = bf16[1,128,4096]{1,2,0:T(8,128)(2,1)S(1)} collective-permute-done((bf16[1,128,4096]{1,2,0:T(8,128)(2,1)S(1)}, bf16[1,128,4096]{1,2,0:T(8,128)(2,1)S(1)}, u32[]{:S(2)}, u32[]{:S(2)}) %collective-permute-start.1) | collective-permute-done | bytes 1048608 | tf_op jit(solution)/shard_map/ppermute | solution.py:19
  357.8 1.3 copy.114
  (225 shorter events, 36.3 us)
Async XLA Ops:
  0.0 2.2 copy-start.10
  1.6 1.7 copy-start
  3.0 10.1 %copy-start.2 = (bf16[128,4096]{0,1:T(8,128)(2,1)}, bf16[128,4096]{0,1:T(8,128)(2,1)S(1)}, u32[]{:S(2)}) copy-start(bf16[128,4096]{0,1:T(8,128)(2,1)S(1)} %fusion.220) | copy-start | bytes 3145732
  3.0 5.4 %copy-start.6 = (bf16[1,3,3,4096]{3,2,1,0:T(4,128)(2,1)S(1)}, bf16[1,3,3,4096]{3,2,1,0:T(4,128)(2,1)}, u32[]{:S(2)}) copy-start(bf16[1,3,3,4096]{3,2,1,0:T(4,128)(2,1)} %param.10) | copy-start | bytes 221188
  3.7 8.8 %collective-permute-start = (bf16[2,4096]{1,0:T(2,128)(2,1)S(1)}, bf16[2,4096]{1,0:T(2,128)(2,1)S(1)}, u32[]{:S(2)}, u32[]{:S(2)}) collective-permute-start(bf16[2,4096]{1,0:T(2,128)(2,1)S(1)} %copy.106), channel_id=1, source_target_pairs={{0,1},{1,2},{2,3},{3,4},{4,5},{5,6},{6,7},{7,8},{8,9},{9,10},{10,1... | collective-permute-start | bytes 49160 | tf_op jit(solution)/shard_map/ppermute | solution.py:13
  13.1 5.7 %copy-start.4 = (bf16[2,4096]{0,1:T(8,128)(2,1)}, bf16[2,4096]{0,1:T(8,128)(2,1)S(1)}, u32[]{:S(2)}) copy-start(bf16[2,4096]{0,1:T(8,128)(2,1)S(1)} %copy.107) | copy-start | bytes 49156
  13.1 14.9 %copy-start.12 = (f32[1,64,16]{1,2,0:T(8,128)S(1)}, f32[1,64,16]{1,2,0:T(8,128)}, u32[]{:S(2)}) copy-start(f32[1,64,16]{1,2,0:T(8,128)} %param.13) | copy-start | bytes 12292
  13.1 15.0 %copy-start.13 = (f32[1,64,16]{1,2,0:T(8,128)S(1)}, f32[1,64,16]{1,2,0:T(8,128)}, u32[]{:S(2)}) copy-start(f32[1,64,16]{1,2,0:T(8,128)} %param.12) | copy-start | bytes 12292
  18.7 37.7 %all-to-all-start = ((bf16[64,64,128]{2,1,0:T(8,128)(2,1)}), bf16[64,64,128]{2,1,0:T(8,128)(2,1)}, u32[]{:S(2)}, u32[]{:S(2)}) async-start(bf16[64,64,128]{2,1,0:T(8,128)(2,1)} %bitcast.15), calls=%async_computation | async-start | bytes 2097152 | tf_op jit(solution)/shard_map/all_to_all | solution.py:54
  263.0 8.5 %copy-start.11 = (bf16[1,4096]{1,0:T(2,128)(2,1)S(1)}, bf16[1,4096]{1,0:T(2,128)(2,1)}, u32[]{:S(2)}) copy-start(bf16[1,4096]{1,0:T(2,128)(2,1)} %param.11) | copy-start | bytes 24580
  265.3 34.8 %all-to-all-start.1 = ((bf16[64,2,4096]{2,1,0:T(2,128)(2,1)}), bf16[64,2,4096]{2,1,0:T(2,128)(2,1)S(1)}, u32[]{:S(2)}, u32[]{:S(2)}) async-start(bf16[64,2,4096]{2,1,0:T(2,128)(2,1)} %reshape.1506), calls=%async_computation.1 | async-start | bytes 2097152 | tf_op jit(solution)/shard_map/all_to_all | solution.py:111
  315.7 1.3 copy-start.1
  315.8 1.5 copy-start.3
  315.8 1.8 copy-start.5
  315.8 1.8 copy-start.7
  315.8 1.8 copy-start.8
  315.8 1.8 copy-start.9
  323.7 34.1 %collective-permute-start.1 = (bf16[1,128,4096]{1,2,0:T(8,128)(2,1)S(1)}, bf16[1,128,4096]{1,2,0:T(8,128)(2,1)S(1)}, u32[]{:S(2)}, u32[]{:S(2)}) collective-permute-start(bf16[1,128,4096]{1,2,0:T(8,128)(2,1)S(1)} %bitcast.381), channel_id=1, source_target_pairs={{448,0},{0,64},{64,128},{128,192},{192,256},{256,320},{320,384},{3... | collective-permute-start | bytes 3145736 | tf_op jit(solution)/shard_map/ppermute | solution.py:19
where the time goes:
time: 363 us; the launch traced here: 359 us
  matrix products  114 us (31%)
  waiting for transfers between devices  90.3 us (25%)
  other arithmetic  64.3 us (18%)
  local copies, waits for them, and re-layouts  37.6 us (10%)
  loops' own time  28.4 us (8%)
  starting transfers between devices  24.1 us (7%)
    dot_general x4, matrix products, one_group(): jnp.einsum('ckb,bq->ckq', turned_real, sin_cols, precision=HIGHEST_PRECIS...  48.8 us
    unnamed x2, other arithmetic  45.3 us
    ppermute x1, waiting for transfers between devices, from_behind_2(): return lax.ppermute(block, axis, route)  30.1 us
    all_to_all x1, waiting for transfers between devices, spectral_conv(): lax.all_to_all(convolved.reshape(1, local_channels, sequence), 'ctx', spl...  28.5 us
    another operation x1, loops' own time, spectral_conv(): convolved = lax.map(one_group, (grouped_lines, time_groups, residue_groups))  28.4 us
    all_to_all x1, waiting for transfers between devices, spectral_conv(): lax.all_to_all(pieces, 'ctx', split_axis=0, concat_axis=2, tiled=True)[0]  28.3 us
    unnamed x33, local copies, waits for them, and re-layouts  12.4 us
    all_to_all x1, starting transfers between devices, spectral_conv(): lax.all_to_all(pieces, 'ctx', split_axis=0, concat_axis=2, tiled=True)[0]  9.25 us
  transfers between devices with their start and end apart: 4, of which 4 were waited for; matrix products, arithmetic and copies ran while one was open for 0% of the time, Pallas kernels for 0%

commit v1 on v0

--- a/solution.py
+++ b/solution.py
@@ -108,13 +108,11 @@
     time_groups = decay_time.reshape(group_count, group_size, mode_count)
     residue_groups = residue.reshape(group_count, group_size, mode_count)
     convolved = lax.map(one_group, (grouped_lines, time_groups, residue_groups))
-    returned = lax.all_to_all(
-        convolved.reshape(1, local_channels, sequence),
-        "ctx",
-        split_axis=2,
-        concat_axis=0,
-        tiled=True,
-    )
+    x = convolved.reshape(1, local_channels, sequence)
+    n_dev = lax.axis_size("ctx")
+    shards = jnp.stack(jnp.split(x, n_dev, axis=2), axis=0)
+    shards = lax.all_to_all(shards, "ctx", split_axis=0, concat_axis=0)
+    returned = jnp.concatenate(shards, axis=0)
     return jnp.transpose(returned.reshape(channels, length))
 
 

time: 363 us -> 297 us (0.82)
  other arithmetic: 64.3 us -> 19 us
  loops' own time: 28.4 us -> 1.94 us
  local copies, waits for them, and re-layouts: 37.6 us -> 44.7 us
    unnamed x2 -> x0, other arithmetic: 45.3 us -> none
    unnamed x33 -> x92, local copies, waits for them, and re-layouts: 12.4 us -> 39.9 us
    another operation x1, loops' own time: 28.4 us -> 1.94 us  [spectral_conv(): convolved = lax.map(one_group, (grouped_lines, time_groups, residue_groups))]
    all_to_all x1 -> x0, local copies, waits for them, and re-layouts: 8.16 us -> none  [spectral_conv(): lax.all_to_all(convolved.reshape(1, local_channels, sequence), 'ctx', spl...]
    reshape x2 -> x1, local copies, waits for them, and re-layouts: 8.35 us -> 0.49 us  [spectral_conv(): x = convolved.reshape(1, local_channels, sequence)]
    dynamic_slice x8, local copies, waits for them, and re-layouts: 3.99 us -> 0.25 us  [spectral_conv(): convolved = lax.map(one_group, (grouped_lines, time_groups, residue_groups))]
where the time goes in v1:
time: 297 us; the launch traced here: 293 us
  matrix products  112 us (38%)
  waiting for transfers between devices  90.3 us (30%)
  local copies, waits for them, and re-layouts  44.7 us (15%)
  starting transfers between devices  24.4 us (8%)
  other arithmetic  19 us (6%)
    dot_general x4, matrix products, one_group(): jnp.einsum('ckb,bq->ckq', turned_real, sin_cols, precision=HIGHEST_PRECIS...  48.9 us
    unnamed x92, local copies, waits for them, and re-layouts  39.9 us
    ppermute x1, waiting for transfers between devices, from_behind_2(): return lax.ppermute(block, axis, route)  30.1 us
    all_to_all x1, waiting for transfers between devices, spectral_conv(): shards = lax.all_to_all(shards, 'ctx', split_axis=0, concat_axis=0)  28.4 us
    all_to_all x1, waiting for transfers between devices, spectral_conv(): lax.all_to_all(pieces, 'ctx', split_axis=0, concat_axis=2, tiled=True)[0]  28.3 us
    all_to_all x1, starting transfers between devices, spectral_conv(): lax.all_to_all(pieces, 'ctx', split_axis=0, concat_axis=2, tiled=True)[0]  9.19 us
    dot_general x4, matrix products, one_group(): jnp.einsum('ckb,bq->ckq', turned_imag, sin_cols, precision=HIGHEST_PRECIS...  8.12 us
    dot_general x4, matrix products, one_group(): jnp.einsum('ckb,bq->ckq', turned_imag, cos_cols, precision=HIGHEST_PRECIS...  8.08 us
  transfers between devices with their start and end apart: 4, of which 4 were waited for; matrix products, arithmetic and copies ran while one was open for 0% of the time, Pallas kernels for 0%

profile of v1, /device:TPU:1, one launch (start us, length us, event | category | flops | bytes accessed | tf_op | source)
XLA Modules:
  0.0 293.1 jit_solution(16925029185464831906)
XLA Ops:
  0.0 1.6 copy.107
  3.9 4.6 %collective-permute-start = (bf16[2,4096]{1,0:T(2,128)(2,1)S(1)}, bf16[2,4096]{1,0:T(2,128)(2,1)S(1)}, u32[]{:S(2)}, u32[]{:S(2)}) collective-permute-start(bf16[2,4096]{1,0:T(2,128)(2,1)S(1)} %copy.108), channel_id=1, source_target_pairs={{0,1},{1,2},{2,3},{3,4},{4,5},{5,6},{6,7},{7,8},{8,9},{9,10},{10,1... | collective-permute-start | bytes 49160 | tf_op jit(solution)/shard_map/ppermute | solution.py:13
  9.2 3.5 %collective-permute-done = bf16[2,4096]{1,0:T(2,128)(2,1)S(1)} collective-permute-done((bf16[2,4096]{1,0:T(2,128)(2,1)S(1)}, bf16[2,4096]{1,0:T(2,128)(2,1)S(1)}, u32[]{:S(2)}, u32[]{:S(2)}) %collective-permute-start) | collective-permute-done | bytes 16416 | tf_op jit(solution)/shard_map/ppermute | solution.py:13
  13.2 5.6 %fusion.215 = bf16[128,4096]{0,1:T(8,128)(2,1)} fusion(bf16[128,4096]{0,1:T(8,128)(2,1)S(1)} %fusion.220, f32[4096]{0:T(1024)S(1)} %bitcast.636, f32[4096]{0:T(1024)S(1)} %bitcast.637, f32[4096]{0:T(1024)S(1)} %bitcast.638, f32[4096]{0:T(1024)S(1)} %bitcast.639, f32[4096]{0:T(1024)S(1)} %bitcast.640, f32[4096]{0:T(1024)S(1)} %bitcast.641, ...), kind=kLoop, calls=%fused_computation.400 | loop fusion | flops 11010048 | bytes 2211840 | tf_op jit(solution)/shard_map/convert_element_type | solution.py:139
  18.8 9.2 %all-to-all-start = ((bf16[64,64,128]{2,1,0:T(8,128)(2,1)}), bf16[64,64,128]{2,1,0:T(8,128)(2,1)S(1)}, u32[]{:S(2)}, u32[]{:S(2)}) async-start(bf16[64,64,128]{2,1,0:T(8,128)(2,1)} %bitcast.15), calls=%async_computation | async-start | bytes 2097152 | tf_op jit(solution)/shard_map/all_to_all | solution.py:54
  28.2 28.3 %all-to-all-done = bf16[64,64,128]{2,1,0:T(8,128)(2,1)S(1)} async-done(((bf16[64,64,128]{2,1,0:T(8,128)(2,1)}), bf16[64,64,128]{2,1,0:T(8,128)(2,1)S(1)}, u32[]{:S(2)}, u32[]{:S(2)}) %all-to-all-start) | async-done | bytes 1048608 | tf_op jit(solution)/shard_map/all_to_all | solution.py:54
  56.6 120.3 %while.18 = (s32[]{:T(128)}, bf16[4,16,64,128]{3,2,1,0:T(8,128)(2,1)S(1)}, bf16[4,16,64,128]{3,1,0,2:T(8,128)(2,1)S(1)}, f32[4,16,16]{1,0,2:T(4,128)S(1)}, f32[4...) while((s32[]{:T(128)}, bf16[4,16,64,128]{3,2,1,0:T(8,128)(2,1)S(1)}, ...), condition=%wide.region_2.3_spmd.clone.clone.clone, body=%wide.region_1.2_spmd.clone.clone.clone.sunk | while | flops 4104389632 | bytes 44585048 | solution.py:110
  58.8 2.0 fusion.277
  60.8 2.0 convolution_add_fusion.4
  63.4 2.0 fusion.281
  66.0 12.2 %multiply_subtract_fusion.9 = (f32[16,128,128]{2,1,0:T(8,128)S(1)}, f32[16,128,128]{2,1,0:T(8,128)S(1)}, f32[16,128,128]{2,1,0:T(8,128)S(1)}, f32[16,128,128]{2,1,0:T(8,128)S(1)}) fusion(f32[16,128,128]{2,1,0:T(8,128)S(1)} %convolution_add_fusion.4, f32[16]{0:T(128)S(1)} %broadcast_multiply_fusion.32, f32[16]{0:T(128)S(1)} %get-tuple-element.1211, ...), kind=kOutput, calls=%fused_computation.108.clone.1 | convolution fusion | flops 471564288 | bytes 8721408 | tf_op jit(solution)/shard_map/while/body/eval_jaxpr/ckb,bq->ckq/dot_general | solution.py:88
  78.2 1.3 fusion.283
  79.8 1.4 convolution_subtract_fusion.4
  82.5 1.4 convolution_add_fusion.5
  83.9 1.5 fusion.284
  85.4 1.5 fusion.285
  88.7 2.0 fusion.277
  90.8 2.0 convolution_add_fusion.4
  93.3 2.0 fusion.281
  95.9 12.2 %multiply_subtract_fusion.9 = (f32[16,128,128]{2,1,0:T(8,128)S(1)}, f32[16,128,128]{2,1,0:T(8,128)S(1)}, f32[16,128,128]{2,1,0:T(8,128)S(1)}, f32[16,128,128]{2,1,0:T(8,128)S(1)}) fusion(f32[16,128,128]{2,1,0:T(8,128)S(1)} %convolution_add_fusion.4, f32[16]{0:T(128)S(1)} %broadcast_multiply_fusion.32, f32[16]{0:T(128)S(1)} %get-tuple-element.1211, ...), kind=kOutput, calls=%fused_computation.108.clone.1 | convolution fusion | flops 471564288 | bytes 8721408 | tf_op jit(solution)/shard_map/while/body/eval_jaxpr/ckb,bq->ckq/dot_general | solution.py:88
  108.2 1.3 fusion.283
  109.8 1.4 convolution_subtract_fusion.4
  112.4 1.4 convolution_add_fusion.5
  113.8 1.5 fusion.284
  115.3 1.5 fusion.285
  118.7 2.0 fusion.277
  120.7 2.0 convolution_add_fusion.4
  123.2 2.0 fusion.281
  125.9 12.2 %multiply_subtract_fusion.9 = (f32[16,128,128]{2,1,0:T(8,128)S(1)}, f32[16,128,128]{2,1,0:T(8,128)S(1)}, f32[16,128,128]{2,1,0:T(8,128)S(1)}, f32[16,128,128]{2,1,0:T(8,128)S(1)}) fusion(f32[16,128,128]{2,1,0:T(8,128)S(1)} %convolution_add_fusion.4, f32[16]{0:T(128)S(1)} %broadcast_multiply_fusion.32, f32[16]{0:T(128)S(1)} %get-tuple-element.1211, ...), kind=kOutput, calls=%fused_computation.108.clone.1 | convolution fusion | flops 471564288 | bytes 8721408 | tf_op jit(solution)/shard_map/while/body/eval_jaxpr/ckb,bq->ckq/dot_general | solution.py:88
  138.1 1.3 fusion.283
  139.7 1.4 convolution_subtract_fusion.4
  142.4 1.4 convolution_add_fusion.5
  143.7 1.5 fusion.284
  145.2 1.5 fusion.285
  148.6 2.0 fusion.277
  150.6 2.0 convolution_add_fusion.4
  153.2 2.0 fusion.281
  155.8 12.2 %multiply_subtract_fusion.9 = (f32[16,128,128]{2,1,0:T(8,128)S(1)}, f32[16,128,128]{2,1,0:T(8,128)S(1)}, f32[16,128,128]{2,1,0:T(8,128)S(1)}, f32[16,128,128]{2,1,0:T(8,128)S(1)}) fusion(f32[16,128,128]{2,1,0:T(8,128)S(1)} %convolution_add_fusion.4, f32[16]{0:T(128)S(1)} %broadcast_multiply_fusion.32, f32[16]{0:T(128)S(1)} %get-tuple-element.1211, ...), kind=kOutput, calls=%fused_computation.108.clone.1 | convolution fusion | flops 471564288 | bytes 8721408 | tf_op jit(solution)/shard_map/while/body/eval_jaxpr/ckb,bq->ckq/dot_general | solution.py:88
  169.7 1.4 convolution_subtract_fusion.4
  172.3 1.4 convolution_add_fusion.5
  173.7 1.5 fusion.284
  175.2 1.5 fusion.285
  216.1 6.5 %all-to-all-start.1 = ((bf16[64,1,64,128]{3,2,1,0:T(8,128)(2,1)}), bf16[64,1,64,128]{3,2,1,0:T(8,128)(2,1)}, u32[]{:S(2)}, u32[]{:S(2)}) async-start(bf16[64,1,64,128]{3,2,1,0:T(8,128)(2,1)} %constant_dynamic-update-slice_fusion), calls=%async_computation.1 | async-start | bytes 2097152 | tf_op jit(solution)/shard_map/all_to_all | solution.py:114
  222.7 28.4 %all-to-all-done.1 = bf16[64,1,64,128]{3,2,1,0:T(8,128)(2,1)} async-done(((bf16[64,1,64,128]{3,2,1,0:T(8,128)(2,1)}), bf16[64,1,64,128]{3,2,1,0:T(8,128)(2,1)}, u32[]{:S(2)}, u32[]{:S(2)}) %all-to-all-start.1) | async-done | bytes 1048608 | tf_op jit(solution)/shard_map/all_to_all | solution.py:114
  251.2 6.3 %fusion.221 = bf16[128,4096]{0,1:T(8,128)(2,1)S(1)} fusion(bf16[128,4096]{0,1:T(8,128)(2,1)S(1)} %copy-done.3, bf16[128,4096]{0,1:T(8,128)(2,1)} %fusion.215, bf16[64,1,64,128]{3,2,1,0:T(8,128)(2,1)} %all-to-all-done.1, bf16[1,128,4096]{1,2,0:T(8,128)(2,1)S(1)} %copy-done.1, f32[4096]{0:T(1024)S(1)} %bitcast.642, f32[4096]{0:T(1024)S(1)} %bitcast.634, ...), kind=kLoop, calls=%fused_computation.406 | loop fusion | flops 11534336 | bytes 5324800 | tf_op jit(solution)/shard_map/convert_element_type | solution.py:142
  257.5 4.0 %collective-permute-start.1 = (bf16[1,128,4096]{1,2,0:T(8,128)(2,1)S(1)}, bf16[1,128,4096]{1,2,0:T(8,128)(2,1)S(1)}, u32[]{:S(2)}, u32[]{:S(2)}) collective-permute-start(bf16[1,128,4096]{1,2,0:T(8,128)(2,1)S(1)} %bitcast.628), channel_id=1, source_target_pairs={{448,0},{0,64},{64,128},{128,192},{192,256},{256,320},{320,384},{3... | collective-permute-start | bytes 3145736 | tf_op jit(solution)/shard_map/ppermute | solution.py:19
  261.5 30.1 %collective-permute-done.1 = bf16[1,128,4096]{1,2,0:T(8,128)(2,1)S(1)} collective-permute-done((bf16[1,128,4096]{1,2,0:T(8,128)(2,1)S(1)}, bf16[1,128,4096]{1,2,0:T(8,128)(2,1)S(1)}, u32[]{:S(2)}, u32[]{:S(2)}) %collective-permute-start.1) | collective-permute-done | bytes 1048608 | tf_op jit(solution)/shard_map/ppermute | solution.py:19
  291.6 1.3 copy.113
  (280 shorter events, 61.2 us)
Async XLA Ops:
  1.6 1.5 copy-start
  1.6 0.7 copy-start.10
  3.1 10.1 %copy-start.2 = (bf16[128,4096]{0,1:T(8,128)(2,1)}, bf16[128,4096]{0,1:T(8,128)(2,1)S(1)}, u32[]{:S(2)}) copy-start(bf16[128,4096]{0,1:T(8,128)(2,1)S(1)} %fusion.220) | copy-start | bytes 3145732
  3.5 5.0 %copy-start.6 = (bf16[1,3,3,4096]{3,2,1,0:T(4,128)(2,1)S(1)}, bf16[1,3,3,4096]{3,2,1,0:T(4,128)(2,1)}, u32[]{:S(2)}) copy-start(bf16[1,3,3,4096]{3,2,1,0:T(4,128)(2,1)} %param.10) | copy-start | bytes 221188
  3.9 8.8 %collective-permute-start = (bf16[2,4096]{1,0:T(2,128)(2,1)S(1)}, bf16[2,4096]{1,0:T(2,128)(2,1)S(1)}, u32[]{:S(2)}, u32[]{:S(2)}) collective-permute-start(bf16[2,4096]{1,0:T(2,128)(2,1)S(1)} %copy.108), channel_id=1, source_target_pairs={{0,1},{1,2},{2,3},{3,4},{4,5},{5,6},{6,7},{7,8},{8,9},{9,10},{10,1... | collective-permute-start | bytes 49160 | tf_op jit(solution)/shard_map/ppermute | solution.py:13
  13.2 5.6 %copy-start.4 = (bf16[2,4096]{0,1:T(8,128)(2,1)}, bf16[2,4096]{0,1:T(8,128)(2,1)S(1)}, u32[]{:S(2)}) copy-start(bf16[2,4096]{0,1:T(8,128)(2,1)S(1)} %copy.109) | copy-start | bytes 49156
  18.8 9.2 %copy-start.12 = (f32[1,64,16]{1,2,0:T(8,128)S(1)}, f32[1,64,16]{1,2,0:T(8,128)}, u32[]{:S(2)}) copy-start(f32[1,64,16]{1,2,0:T(8,128)} %param.13) | copy-start | bytes 12292
  18.8 9.3 %copy-start.13 = (f32[1,64,16]{1,2,0:T(8,128)S(1)}, f32[1,64,16]{1,2,0:T(8,128)}, u32[]{:S(2)}) copy-start(f32[1,64,16]{1,2,0:T(8,128)} %param.12) | copy-start | bytes 12292
  18.8 37.8 %all-to-all-start = ((bf16[64,64,128]{2,1,0:T(8,128)(2,1)}), bf16[64,64,128]{2,1,0:T(8,128)(2,1)S(1)}, u32[]{:S(2)}, u32[]{:S(2)}) async-start(bf16[64,64,128]{2,1,0:T(8,128)(2,1)} %bitcast.15), calls=%async_computation | async-start | bytes 2097152 | tf_op jit(solution)/shard_map/all_to_all | solution.py:54
  195.5 27.1 %copy-start.11 = (bf16[1,4096]{1,0:T(2,128)(2,1)S(1)}, bf16[1,4096]{1,0:T(2,128)(2,1)}, u32[]{:S(2)}) copy-start(bf16[1,4096]{1,0:T(2,128)(2,1)} %param.11) | copy-start | bytes 24580
  195.5 55.6 %copy-start.9 = (f32[1,1,4096]{2,1,0:T(1,128)S(1)}, f32[1,1,4096]{2,1,0:T(1,128)}, u32[]{:S(2)}) copy-start(f32[1,1,4096]{2,1,0:T(1,128)} %get-tuple-element.1078) | copy-start | bytes 49156
  196.7 54.4 %copy-start.5 = (bf16[2,4096]{0,1:T(8,128)(2,1)S(1)}, bf16[2,4096]{0,1:T(8,128)(2,1)}, u32[]{:S(2)}) copy-start(bf16[2,4096]{0,1:T(8,128)(2,1)} %copy-done.4) | copy-start | bytes 49156
  216.1 35.0 %copy-start.1 = (bf16[1,128,4096]{1,2,0:T(8,128)(2,1)S(1)}, bf16[1,128,4096]{1,2,0:T(8,128)(2,1)}, u32[]{:S(2)}) copy-start(bf16[1,128,4096]{1,2,0:T(8,128)(2,1)} %copy-done) | copy-start | bytes 3145732
  216.1 35.0 %copy-start.3 = (bf16[128,4096]{0,1:T(8,128)(2,1)S(1)}, bf16[128,4096]{0,1:T(8,128)(2,1)}, u32[]{:S(2)}) copy-start(bf16[128,4096]{0,1:T(8,128)(2,1)} %copy-done.2) | copy-start | bytes 3145732
  216.1 35.0 %copy-start.7 = (f32[1,1,4096]{2,1,0:T(1,128)S(1)}, f32[1,1,4096]{2,1,0:T(1,128)}, u32[]{:S(2)}) copy-start(f32[1,1,4096]{2,1,0:T(1,128)} %get-tuple-element.1070) | copy-start | bytes 49156
  216.1 35.0 %copy-start.8 = (f32[1,1,4096]{2,1,0:T(1,128)S(1)}, f32[1,1,4096]{2,1,0:T(1,128)}, u32[]{:S(2)}) copy-start(f32[1,1,4096]{2,1,0:T(1,128)} %get-tuple-element.1077) | copy-start | bytes 49156
  216.1 35.0 %all-to-all-start.1 = ((bf16[64,1,64,128]{3,2,1,0:T(8,128)(2,1)}), bf16[64,1,64,128]{3,2,1,0:T(8,128)(2,1)}, u32[]{:S(2)}, u32[]{:S(2)}) async-start(bf16[64,1,64,128]{3,2,1,0:T(8,128)(2,1)} %constant_dynamic-update-slice_fusion), calls=%async_computation.1 | async-start | bytes 2097152 | tf_op jit(solution)/shard_map/all_to_all | solution.py:114
  257.5 34.1 %collective-permute-start.1 = (bf16[1,128,4096]{1,2,0:T(8,128)(2,1)S(1)}, bf16[1,128,4096]{1,2,0:T(8,128)(2,1)S(1)}, u32[]{:S(2)}, u32[]{:S(2)}) collective-permute-start(bf16[1,128,4096]{1,2,0:T(8,128)(2,1)S(1)} %bitcast.628), channel_id=1, source_target_pairs={{448,0},{0,64},{64,128},{128,192},{192,256},{256,320},{320,384},{3... | collective-permute-start | bytes 3145736 | tf_op jit(solution)/shard_map/ppermute | solution.py:19
